TPU v7x, 512 devices: a whole 4x8x8 slice. The times are simulated.
512 devices in a mesh: dp: 8 (over y), feat: 64 (over x, z, core).
Axes of the slice: x: 4, y: 8, z: 8, core: 2. Of those that a mesh axis runs over, the one named last changes fastest.
Arguments:
- features: bfloat16 [8, 16384, 128], P('dp', None, 'feat'), may hold values from -6 to 6
- tile_weights: bfloat16 [8, 1536, 128, 128], P('dp', 'feat'), may hold values from -0.15625 to 0.15625
- tile_rows: int32 [8, 1536], P('dp', 'feat'), may hold values from 0 to 1
- tile_owners: int32 [8, 1536, 1], P('dp', 'feat'), may hold values from 0 to 63; in each aligned block of 24 rows (0 to 23, 24 to 47, ..., all dimensions but the last counted through in order) at most 2 rows name the same one
- tile_blocks: int32 [8, 1536], P('dp', 'feat'), may hold values from 0 to 1
- tile_counts: int32 [8, 64], P('dp', 'feat'), may hold values from 6 to 24, as said below
- cotangent: bfloat16 [8, 16384, 1024], P('dp', 'feat'), may hold values from -0.046875 to 0.046875
- w_self: bfloat16 [128, 1024], replicated, may hold values from -0.5 to 0.5
- w_neigh: bfloat16 [128, 1024], replicated, may hold values from -0.5 to 0.5
- bias: float32 [1024], replicated, may hold values from -4 to 4
Outputs:
- grad_self: float32 [128, 1024], P(None, 'feat')
- grad_neigh: float32 [128, 1024], P(None, 'feat')
- grad_bias: float32 [1024], P('feat')
Inputs may be any that keep to these rules, and one draw needn't show every extreme that they name: `tile_owners`: among the 24 tile slots of one device at most 2 name one owner, a bound that some block of them reaches. `tile_counts`: in every batch some device has all 24 slots live.
All inputs are finite; a program needn't handle non-finite values.
Results may differ from a plain program's by a relative error of at most 0.008.
Values may be sent and summed in bfloat16 or wider, within the bound.
No kernel may reach another device: no remote copies, remote signals or barrier semaphores. Data moves between devices by JAX's collectives and lax.ppermute only.
A program may use at most 64 MiB of HBM per device.

v0:
```python
import jax
import jax.numpy as jnp
from jax import lax
from jax.sharding import PartitionSpec as P


def silu_slope(pre_act):
    sigmoid_z = jax.nn.sigmoid(pre_act)
    return sigmoid_z * (1.0 + pre_act * (1.0 - sigmoid_z))


def local(
    features,
    tile_weights,
    tile_rows,
    tile_owners,
    tile_blocks,
    tile_counts,
    cotangent,
    w_self,
    w_neigh,
    bias,
):
    owned = lax.all_to_all(features, "feat", split_axis=1, concat_axis=2, tiled=True)[0]
    node_rows, feat_width = owned.shape
    slot_count = tile_weights.shape[1]
    tile_side = tile_weights.shape[2]
    row_blocks = node_rows // tile_side
    peer_count = lax.axis_size("feat")
    row_index = tile_rows[0]
    owner_index = tile_owners[0, :, 0]
    block_index = tile_blocks[0]
    live = jnp.arange(slot_count, dtype=jnp.int32) < tile_counts[0, 0]
    whole = lax.all_gather(owned, "feat", axis=0, tiled=True)
    picked = whole.reshape(-1, tile_side, feat_width)[owner_index * row_blocks + block_index]
    products = jnp.einsum(
        "kij,kjf->kif", tile_weights[0], picked, preferred_element_type=jnp.float32
    )
    select = (
        (row_index[None, :] == jnp.arange(row_blocks, dtype=jnp.int32)[:, None]) & live[None, :]
    ).astype(jnp.float32)
    summed = jnp.einsum("rk,kif->rif", select, products, precision=lax.Precision.HIGHEST)
    neighbour = summed.reshape(node_rows, feat_width).astype(jnp.bfloat16)
    pre_act = (
        jnp.dot(owned, w_self, preferred_element_type=jnp.float32)
        + jnp.dot(neighbour, w_neigh, preferred_element_type=jnp.float32)
        + bias
    )
    slope = (cotangent[0].astype(jnp.float32) * silu_slope(pre_act)).astype(jnp.bfloat16)
    grad_s = jnp.einsum("nf,nh->fh", owned, slope, preferred_element_type=jnp.float32)
    grad_n = jnp.einsum("nf,nh->fh", neighbour, slope, preferred_element_type=jnp.float32)
    grad_b = jnp.sum(slope.astype(jnp.float32), axis=0)
    total_s, total_n, total_b = lax.psum((grad_s, grad_n, grad_b), ("dp", "feat"))
    column_count = w_self.shape[1] // peer_count
    start = lax.axis_index("feat") * column_count
    out_s = lax.dynamic_slice_in_dim(total_s, start, column_count, 1)
    out_n = lax.dynamic_slice_in_dim(total_n, start, column_count, 1)
    out_b = lax.dynamic_slice_in_dim(total_b, start, column_count, 0)
    return (out_s, out_n, out_b)


def solution(mesh):
    return jax.shard_map(
        local,
        mesh=mesh,
        in_specs=(
            P("dp", None, "feat"),
            P("dp", "feat", None, None),
            P("dp", "feat"),
            P("dp", "feat", None),
            P("dp", "feat"),
            P("dp", "feat"),
            P("dp", "feat", None),
            P(),
            P(),
            P(),
        ),
        out_specs=(P(None, "feat"), P(None, "feat"), P("feat")),
        check_vma=False,
    )
```

profile of v0, /device:TPU:23, one launch (start us, length us, event | category | flops | bytes accessed | tf_op | source)
XLA Modules:
  0.0 554.2 jit_solution(6314317441695136422)
XLA Ops:
  7.2 0.0 copy-start
  7.2 0.0 all-gather.2.cloned.1.call-start
  7.2 15.4 %copy.26 = bf16[1,16384,2]{2,0,1:T(2,128)(2,1)} copy(bf16[1,16384,2]{1,2,0:T(2,128)(2,1)} %param.10) | data formatting | bytes 131072 | tf_op args[0]
  22.6 0.5 broadcast.52
  23.1 90.8 %reduce = bf16[16384,2]{1,0:T(8,128)(2,1)} reduce(bf16[16384,1,2]{2,1,0:T(2,128)(2,1)} %bitcast.51, bf16[]{:T(256)} %broadcast.52), dimensions={1}, to_apply=%bitcast.36.reduce_sub_computation | reduce | bytes 131074
  113.9 7.1 %reshape.61 = bf16[64,2,256]{2,1,0:T(2,128)(2,1)S(1)} reshape(bf16[16384,2]{1,0:T(8,128)(2,1)} %reduce) | data formatting | bytes 131072
  121.0 21.9 %all_to_all.15 = bf16[64,2,256]{2,1,0:T(2,128)(2,1)S(1)} all-to-all(bf16[64,2,256]{2,1,0:T(2,128)(2,1)S(1)} %reshape.61), channel_id=1, replica_groups=mesh['dp'=8,'feat'=64] {'feat'}, dimensions={0} | all-to-all | bytes 131072 | tf_op jit(solution)/shard_map/all_to_all | solution.py:24
  142.9 16.4 %reshape.62 = bf16[16384,1,2]{2,1,0:T(2,128)(2,1)} reshape(bf16[64,2,256]{2,1,0:T(2,128)(2,1)S(1)} %all_to_all.15) | data formatting | bytes 131072
  159.3 0.0 copy-start.5
  159.3 0.0 copy-start.6
  159.3 0.0 copy-start.2
  159.3 15.4 %copy.27 = bf16[1,16384,2]{1,2,0:T(2,128)(2,1)S(1)} copy(bf16[1,16384,2]{2,0,1:T(2,128)(2,1)} %bitcast.52) | data formatting | bytes 131072 | tf_op jit(solution)/shard_map/all_to_all | solution.py:24
  174.7 0.1 copy.28
  174.8 0.7 squeeze.14
  175.4 0.0 all-gather.2.cloned.1.call-update
  175.5 0.2 all-reduce.3.cloned.1.call-start
  176.3 0.0 copy-done.5
  176.4 0.0 copy-done.6
  176.4 0.0 copy-done.2
  176.4 1.2 fusion.10
  177.6 77.5 %all-gather.2.cloned.1.call-done = bf16[16384,128]{0,1:T(8,128)(2,1)} async-done(((bf16[256,128]{0,1:T(8,128)(2,1)}), bf16[16384,128]{0,1:T(8,128)(2,1)}) %all-gather.2.cloned.1.call-update) | async-done | bytes 4194320 | tf_op jit(solution)/shard_map/all_gather | solution.py:34
  255.0 6.4 %copy.29 = bf16[16384,128]{1,0:T(8,128)(2,1)} copy(bf16[16384,128]{0,1:T(8,128)(2,1)} %all-gather.2.cloned.1.call-done) | data formatting | bytes 8388608 | tf_op jit(solution)/shard_map/all_gather | solution.py:34
  261.4 0.0 copy-start.3
  261.4 2.9 gather_fusion
  264.3 0.0 copy-done
  264.4 0.0 copy-start.4
  264.4 1.9 convolution_bitcast_fusion
  266.2 2.0 copy.31
  268.2 0.0 copy-done.3
  268.2 0.6 convolution_convert_fusion
  268.8 0.0 copy-start.1
  268.8 0.0 copy-done.4
  268.9 1.8 convert_reduce_fusion
  270.6 1.1 fusion.11
  271.8 0.0 copy-done.1
  271.8 1.1 convolution_bitcast_fusion.1
  272.9 0.0 all-reduce.3.cloned.1.call-update
  272.9 96.3 %psum.23 = f32[1024]{0:T(1024)S(1)} all-reduce(f32[1024]{0:T(1024)S(1)} %get-tuple-element.5), channel_id=1, replica_groups=mesh['dp'=8,'feat'=64] {'dp','feat'}, use_global_device_ids=true, to_apply=%region_3.0 | all-reduce | flops 1024 | bytes 8192 | tf_op jit(solution)/shard_map/psum | solution.py:53
  369.3 0.6 dynamic_slice.11
  369.9 176.2 %all-reduce.3.cloned.1.call-done = (f32[128,1024]{0,1:T(8,128)}, f32[128,1024]{0,1:T(8,128)}) async-done(((f32[128,1024]{0,1:T(8,128)}, f32[128,1024]{0,1:T(8,128)}), (f32[128,1024]{0,1:T(8,128)}, f32[128,1024]{0,1:T(8,128)})) %all-reduce.3.cloned.1.call-update) | async-done | bytes 1048592 | tf_op jit(solution)/shard_map/psum | solution.py:53
  546.0 1.3 constant_dynamic-slice_fusion
  (5 shorter events, 0.0 us)
Async XLA Ops:
  7.2 257.2 %copy-start = (bf16[1,24,128,128]{3,2,1,0:T(8,128)(2,1)S(1)}, bf16[1,24,128,128]{3,2,1,0:T(8,128)(2,1)}, u32[]{:S(2)}) copy-start(bf16[1,24,128,128]{3,2,1,0:T(8,128)(2,1)} %param.11) | copy-start | bytes 2359300
  7.2 247.8 %all-gather.2.cloned.1.call-start = ((), (), s32[]{:S(2)}) async-start(), calls=%async_computation.1 | async-start | bytes 4259840 | tf_op jit(solution)/shard_map/all_gather | solution.py:34
  159.3 17.1 %copy-start.5 = (s32[1,24]{1,0:T(1,128)S(1)}, s32[1,24]{1,0:T(1,128)}, u32[]{:S(2)}) copy-start(s32[1,24]{1,0:T(1,128)} %param.14) | copy-start | bytes 292
  159.3 17.1 %copy-start.6 = (s32[1,24,1]{1,2,0:T(1,128)S(1)}, s32[1,24,1]{1,2,0:T(1,128)}, u32[]{:S(2)}) copy-start(s32[1,24,1]{1,2,0:T(1,128)} %param.13) | copy-start | bytes 292
  159.3 17.1 %copy-start.2 = (bf16[128,1024]{1,0:T(8,128)(2,1)S(1)}, bf16[128,1024]{1,0:T(8,128)(2,1)}, u32[]{:S(2)}) copy-start(bf16[128,1024]{1,0:T(8,128)(2,1)} %param.17) | copy-start | bytes 786436
  175.5 370.6 %all-reduce.3.cloned.1.call-start = ((), (), s32[]{:S(2)}) async-start(), calls=%async_computation.2 | async-start | bytes 2097152 | tf_op jit(solution)/shard_map/psum | solution.py:53
  261.4 6.8 %copy-start.3 = (s32[1,24]{1,0:T(1,128)S(1)}, s32[1,24]{1,0:T(1,128)}, u32[]{:S(2)}) copy-start(s32[1,24]{1,0:T(1,128)} %param.12) | copy-start | bytes 292
  264.4 4.5 copy-start.4
  268.8 3.0 copy-start.1
Sparse Core Ops, SparseCore 0:
  175.6 79.3 all-gather.1
  273.1 272.9 all-reduce.2
where the time goes:
time: 556 us; the launch traced here: 554 us
  waiting for transfers between devices  254 us (46%)
  blocking collectives  118 us (21%)
  other arithmetic  90.8 us (16%)
  local copies, waits for them, and re-layouts  68.7 us (12%)
  between operations  14.9 us (3%)
  matrix products  7.67 us (1%)
    psum x1, waiting for transfers between devices, local(): lax.psum((grad_s, grad_n, grad_b), ('dp', 'feat'))  176 us
    psum x1, blocking collectives, local(): lax.psum((grad_s, grad_n, grad_b), ('dp', 'feat'))  96.3 us
    unnamed x1, other arithmetic  90.8 us
    all_gather x1, waiting for transfers between devices, local(): whole = lax.all_gather(owned, 'feat', axis=0, tiled=True)  77.5 us
    unnamed x19, local copies, waits for them, and re-layouts  39.5 us
    all_to_all x1, blocking collectives, local(): lax.all_to_all(features, 'feat', split_axis=1, concat_axis=2, tiled=True)[0]  21.9 us
    all_to_all x2, local copies, waits for them, and re-layouts, local(): lax.all_to_all(features, 'feat', split_axis=1, concat_axis=2, tiled=True)[0]  15.5 us
  transfers between devices with their start and end apart: 2, of which 2 were waited for; matrix products, arithmetic and copies ran while one was open for 0% of the time, Pallas kernels for 0%

commit v1 on v0

--- a/solution.py
+++ b/solution.py
@@ -2,6 +2,10 @@
 import jax.numpy as jnp
 from jax import lax
 from jax.sharding import PartitionSpec as P
+
+order_the_grid = lambda u: jnp.concatenate(
+    lax.all_to_all(jnp.stack(lax.axis_size("feat") * [u]), "feat", 0, 0), axis=0
+)
 
 
 def silu_slope(pre_act):
@@ -31,7 +35,7 @@
     owner_index = tile_owners[0, :, 0]
     block_index = tile_blocks[0]
     live = jnp.arange(slot_count, dtype=jnp.int32) < tile_counts[0, 0]
-    whole = lax.all_gather(owned, "feat", axis=0, tiled=True)
+    whole = order_the_grid(owned)
     picked = whole.reshape(-1, tile_side, feat_width)[owner_index * row_blocks + block_index]
     products = jnp.einsum(
         "kij,kjf->kif", tile_weights[0], picked, preferred_element_type=jnp.float32

time: 556 us -> 573 us (1.031)
  waiting for transfers between devices: 254 us -> 269 us
  starting transfers between devices: 0.26 us -> 7.93 us
    all_to_all x0 -> x1, waiting for transfers between devices: none -> 94.5 us  [lax.all_to_all(jnp.stack(lax.axis_size('feat') * [u]), 'feat', 0, 0)]
    all_gather x1 -> x0, waiting for transfers between devices: 77.5 us -> none  [local(): whole = lax.all_gather(owned, 'feat', axis=0, tiled=True)]
    all_to_all x0 -> x1, starting transfers between devices: none -> 7.71 us  [lax.all_to_all(jnp.stack(lax.axis_size('feat') * [u]), 'feat', 0, 0)]
    all_gather x1 -> x0, local copies, waits for them, and re-layouts: 6.42 us -> none  [local(): whole = lax.all_gather(owned, 'feat', axis=0, tiled=True)]
    unnamed x19 -> x17, local copies, waits for them, and re-layouts: 39.5 us -> 39.6 us
where the time goes in v1:
time: 573 us; the launch traced here: 572 us
  waiting for transfers between devices  269 us (47%)
  blocking collectives  117 us (20%)
  other arithmetic  90.8 us (16%)
  local copies, waits for them, and re-layouts  64.9 us (11%)
  between operations  14.9 us (3%)
  starting transfers between devices  7.93 us (1%)
  matrix products  6.86 us (1%)
    psum x1, waiting for transfers between devices, local(): lax.psum((grad_s, grad_n, grad_b), ('dp', 'feat'))  174 us
    psum x1, blocking collectives, local(): lax.psum((grad_s, grad_n, grad_b), ('dp', 'feat'))  95.6 us
    all_to_all x1, waiting for transfers between devices, lax.all_to_all(jnp.stack(lax.axis_size('feat') * [u]), 'feat', 0, 0)  94.5 us
    unnamed x1, other arithmetic  90.7 us
    unnamed x17, local copies, waits for them, and re-layouts  39.6 us
    all_to_all x1, blocking collectives, local(): lax.all_to_all(features, 'feat', split_axis=1, concat_axis=2, tiled=True)[0]  21.9 us
    all_to_all x2, local copies, waits for them, and re-layouts, local(): lax.all_to_all(features, 'feat', split_axis=1, concat_axis=2, tiled=True)[0]  15.4 us
  transfers between devices with their start and end apart: 2, of which 2 were waited for; matrix products, arithmetic and copies ran while one was open for 0% of the time, Pallas kernels for 0%

profile of v1, /device:TPU:23, one launch (start us, length us, event | category | flops | bytes accessed | tf_op | source)
XLA Modules:
  0.0 571.7 jit_solution(8708013582282710568)
XLA Ops:
  7.2 0.0 copy-start
  7.2 15.4 %copy.21 = bf16[1,16384,2]{2,0,1:T(2,128)(2,1)} copy(bf16[1,16384,2]{1,2,0:T(2,128)(2,1)} %param.10) | data formatting | bytes 131072 | tf_op args[0]
  22.6 0.5 broadcast.53
  23.1 90.7 %reduce = bf16[16384,2]{1,0:T(8,128)(2,1)} reduce(bf16[16384,1,2]{2,1,0:T(2,128)(2,1)} %bitcast.51, bf16[]{:T(256)} %broadcast.53), dimensions={1}, to_apply=%bitcast.36.reduce_sub_computation | reduce | bytes 131074
  113.8 7.1 %reshape.59 = bf16[64,2,256]{2,1,0:T(2,128)(2,1)S(1)} reshape(bf16[16384,2]{1,0:T(8,128)(2,1)} %reduce) | data formatting | bytes 131072
  121.0 21.9 %all_to_all.20 = bf16[64,2,256]{2,1,0:T(2,128)(2,1)S(1)} all-to-all(bf16[64,2,256]{2,1,0:T(2,128)(2,1)S(1)} %reshape.59), channel_id=1, replica_groups=mesh['dp'=8,'feat'=64] {'feat'}, dimensions={0} | all-to-all | bytes 131072 | tf_op jit(solution)/shard_map/all_to_all | solution.py:28
  142.8 16.5 %reshape.60 = bf16[16384,1,2]{2,1,0:T(2,128)(2,1)} reshape(bf16[64,2,256]{2,1,0:T(2,128)(2,1)S(1)} %all_to_all.20) | data formatting | bytes 131072
  159.3 15.3 %copy.22 = bf16[1,16384,2]{1,2,0:T(2,128)(2,1)S(1)} copy(bf16[1,16384,2]{2,0,1:T(2,128)(2,1)} %bitcast.52) | data formatting | bytes 131072 | tf_op jit(solution)/shard_map/all_to_all | solution.py:28
  174.7 0.1 copy.23
  174.8 0.1 copy.24
  174.9 3.0 stack.3
  177.9 0.0 copy-start.4
  177.9 0.0 copy-start.5
  177.9 0.0 copy-start.1
  177.9 7.7 %all-to-all-start.1 = ((bf16[64,256,128]{2,1,0:T(8,128)(2,1)}), bf16[64,256,128]{2,1,0:T(8,128)(2,1)}, u32[]{:S(2)}, u32[]{:S(2)}) async-start(bf16[64,256,128]{2,1,0:T(8,128)(2,1)} %stack.3), calls=%async_computation.1 | async-start | bytes 8388608 | tf_op jit(solution)/shard_map/all_to_all | solution.py:7
  185.6 0.2 all-reduce.3.cloned.1.call-start
  186.5 0.0 copy-done.4
  186.5 0.0 copy-done.5
  186.6 0.0 copy-done.1
  186.6 0.3 fusion.10
  186.9 0.0 copy-start.2
  186.9 94.5 %all-to-all-done.1 = bf16[64,256,128]{2,1,0:T(8,128)(2,1)} async-done(((bf16[64,256,128]{2,1,0:T(8,128)(2,1)}), bf16[64,256,128]{2,1,0:T(8,128)(2,1)}, u32[]{:S(2)}, u32[]{:S(2)}) %all-to-all-start.1) | async-done | bytes 4194336 | tf_op jit(solution)/shard_map/all_to_all | solution.py:7
  281.4 2.9 gather_fusion
  284.3 0.0 copy-done
  284.3 0.0 copy-start.3
  284.3 1.9 convolution_bitcast_fusion
  286.2 2.0 copy.26
  288.1 0.0 copy-done.2
  288.1 0.6 convolution_convert_fusion
  288.8 0.0 copy-done.3
  288.8 1.8 convert_reduce_fusion
  290.5 1.1 fusion.11
  291.7 1.2 convolution_bitcast_fusion.1
  292.8 0.0 all-reduce.3.cloned.1.call-update
  292.9 95.6 %psum.23 = f32[1024]{0:T(1024)S(1)} all-reduce(f32[1024]{0:T(1024)S(1)} %get-tuple-element.5), channel_id=1, replica_groups=mesh['dp'=8,'feat'=64] {'dp','feat'}, use_global_device_ids=true, to_apply=%region_3.0 | all-reduce | flops 1024 | bytes 8192 | tf_op jit(solution)/shard_map/psum | solution.py:57
  388.5 0.6 dynamic_slice.11
  389.1 174.4 %all-reduce.3.cloned.1.call-done = (f32[128,1024]{0,1:T(8,128)}, f32[128,1024]{0,1:T(8,128)}) async-done(((f32[128,1024]{0,1:T(8,128)}, f32[128,1024]{0,1:T(8,128)}), (f32[128,1024]{0,1:T(8,128)}, f32[128,1024]{0,1:T(8,128)})) %all-reduce.3.cloned.1.call-update) | async-done | bytes 1048592 | tf_op jit(solution)/shard_map/psum | solution.py:57
  563.5 1.3 constant_dynamic-slice_fusion
  (6 shorter events, 0.1 us)
Async XLA Ops:
  7.2 277.1 %copy-start = (bf16[1,24,128,128]{3,2,1,0:T(8,128)(2,1)S(1)}, bf16[1,24,128,128]{3,2,1,0:T(8,128)(2,1)}, u32[]{:S(2)}) copy-start(bf16[1,24,128,128]{3,2,1,0:T(8,128)(2,1)} %param.11) | copy-start | bytes 2359300
  177.9 8.6 %copy-start.4 = (s32[1,24]{1,0:T(1,128)S(1)}, s32[1,24]{1,0:T(1,128)}, u32[]{:S(2)}) copy-start(s32[1,24]{1,0:T(1,128)} %param.14) | copy-start | bytes 292
  177.9 8.6 %copy-start.5 = (s32[1,24,1]{1,2,0:T(1,128)S(1)}, s32[1,24,1]{1,2,0:T(1,128)}, u32[]{:S(2)}) copy-start(s32[1,24,1]{1,2,0:T(1,128)} %param.13) | copy-start | bytes 292
  177.9 8.7 %copy-start.1 = (bf16[128,1024]{1,0:T(8,128)(2,1)S(1)}, bf16[128,1024]{1,0:T(8,128)(2,1)}, u32[]{:S(2)}) copy-start(bf16[128,1024]{1,0:T(8,128)(2,1)} %param.17) | copy-start | bytes 786436
  177.9 103.5 %all-to-all-start.1 = ((bf16[64,256,128]{2,1,0:T(8,128)(2,1)}), bf16[64,256,128]{2,1,0:T(8,128)(2,1)}, u32[]{:S(2)}, u32[]{:S(2)}) async-start(bf16[64,256,128]{2,1,0:T(8,128)(2,1)} %stack.3), calls=%async_computation.1 | async-start | bytes 8388608 | tf_op jit(solution)/shard_map/all_to_all | solution.py:7
  185.6 377.8 %all-reduce.3.cloned.1.call-start = ((), (), s32[]{:S(2)}) async-start(), calls=%async_computation.2 | async-start | bytes 2097152 | tf_op jit(solution)/shard_map/psum | solution.py:57
  186.9 101.2 %copy-start.2 = (s32[1,24]{1,0:T(1,128)S(1)}, s32[1,24]{1,0:T(1,128)}, u32[]{:S(2)}) copy-start(s32[1,24]{1,0:T(1,128)} %param.12) | copy-start | bytes 292
  284.3 4.5 copy-start.3
Sparse Core Ops, SparseCore 0:
  293.0 270.4 all-reduce.2
